TPU v7x, 32 devices: a whole 2x2x4 slice. The times are simulated.
32 devices in a mesh: ctx: 32 (over z, y, x, core).
Axes of the slice: x: 2, y: 2, z: 4, core: 2. Of those that a mesh axis runs over, the one named last changes fastest.
Arguments:
- query: bfloat16 [8192, 1280], P('ctx'), may hold values from -16 to 16
- key: bfloat16 [8192, 1280], P('ctx'), may hold values from -16 to 16
- value: bfloat16 [8192, 1280], P('ctx'), may hold values from -6 to 6
- grad_out: bfloat16 [8192, 1280], P('ctx'), may hold values from -16 to 16
- offsets: int32 [2, 10], replicated, may hold values from 0 to 255, as said below
Outputs:
- grad_query: bfloat16 [8192, 1280], P('ctx')
- grad_key: bfloat16 [8192, 1280], P('ctx')
- grad_value: bfloat16 [8192, 1280], P('ctx')
Inputs may be any that keep to these rules, and one draw needn't show every extreme that they name: Row 0 holds 0 or 1 for each head, half of the heads taking each; row 1 holds distinct offsets below 256, one of them 256 - 1.
All inputs are finite; a program needn't handle non-finite values.
Results may differ from a plain program's by a relative error of at most 0.007.
Values may be sent and summed in bfloat16 or wider, within the bound.
No kernel may reach another device: no remote copies, remote signals or barrier semaphores. Data moves between devices by JAX's collectives and lax.ppermute only.
A program may use at most 64 MiB of HBM per device.

v0:
```python
import jax
import jax.numpy as jnp
from jax import lax
from jax.sharding import PartitionSpec as P


def swapped(block, axis, bit):
    count = lax.axis_size(axis)
    route = []
    for low in range(count):
        high = low | 1 << bit
        if high != low and high < count:
            route += [(low, high), (high, low)]
    return lax.ppermute(block, axis, route)


def selector_table(dilation, offset_row, dtype):
    return (
        lax.broadcasted_iota(jnp.int32, (dilation, offset_row.shape[0]), 0) == offset_row[None, :]
    ).astype(dtype)


def pick_rows(source, dilation, offset_row):
    length, head_count, head_size = source.shape
    selector = selector_table(dilation, offset_row, source.dtype)
    grouped = source.reshape(length // dilation, dilation, head_count, head_size)
    return jnp.sum(grouped * selector[None, :, :, None], axis=1)


def place_rows(source, dilation, offset_row):
    length, head_count, head_size = source.shape
    selector = selector_table(dilation, offset_row, source.dtype)
    return (source[:, None] * selector[None, :, :, None]).reshape(
        length * dilation, head_count, head_size
    )


def pick_stats(source, dilation, offset_row):
    head_count, length = source.shape
    selector = selector_table(dilation, offset_row, source.dtype)
    grouped = source.reshape(head_count, length // dilation, dilation)
    return jnp.sum(grouped * selector.T[:, None, :], axis=2)


def place_stats(source, dilation, offset_row):
    head_count, length = source.shape
    selector = selector_table(dilation, offset_row, source.dtype)
    return (source[:, :, None] * selector.T[:, None, :]).reshape(head_count, length * dilation)


def forward_level(queries, keys_in, values_in):
    factor = queries.shape[-1] ** (-0.5)
    scores = (
        jnp.einsum("mhc,nhc->hmn", queries, keys_in, preferred_element_type=jnp.float32) * factor
    )
    row_peak = jnp.max(scores, axis=-1)
    powered = jnp.exp(scores - row_peak[:, :, None])
    row_total = jnp.sum(powered, axis=-1)
    blended = jnp.einsum(
        "hmn,nhc->mhc", powered.astype(jnp.bfloat16), values_in, preferred_element_type=jnp.float32
    )
    return (row_peak, row_total, blended)


def backward_level(queries, keys_in, values_in, out_grads, log_total, row_delta):
    factor = queries.shape[-1] ** (-0.5)
    scores = (
        jnp.einsum("mhc,nhc->hmn", queries, keys_in, preferred_element_type=jnp.float32) * factor
    )
    chances = jnp.exp(scores - log_total[:, :, None])
    value_grad = jnp.einsum(
        "hmn,mhc->nhc", chances.astype(jnp.bfloat16), out_grads, preferred_element_type=jnp.float32
    )
    product_grad = jnp.einsum(
        "mhc,nhc->hmn", out_grads, values_in, preferred_element_type=jnp.float32
    )
    score_grad = (factor * chances * (product_grad - row_delta[:, :, None])).astype(jnp.bfloat16)
    query_grad = jnp.einsum("hmn,nhc->mhc", score_grad, keys_in, preferred_element_type=jnp.float32)
    key_grad = jnp.einsum("hmn,mhc->nhc", score_grad, queries, preferred_element_type=jnp.float32)
    return (query_grad, key_grad, value_grad)


def on_device(query, key, value, grad_out, offsets):
    length = query.shape[0]
    head_count = offsets.shape[1]
    head_size = query.shape[1] // head_count
    queries, keys_own, values_own, out_grads = [
        operand.reshape(length, head_count, head_size) for operand in (query, key, value, grad_out)
    ]
    span = min(lax.axis_size("ctx"), 128)
    doublings = span.bit_length() - 1
    pair_offsets = offsets[0]
    wide_offsets = offsets[1]
    half_rows = length // 2
    pair_parts = [
        pick_rows(operand, 2, pair_offsets)
        for operand in (keys_own, values_own, queries, out_grads)
    ]
    wide_parts = [
        pick_rows(operand, length, wide_offsets)
        for operand in (keys_own, values_own, queries, out_grads)
    ]
    pair_load = jnp.stack(pair_parts[:2], 1)
    wide_load = jnp.stack(wide_parts[:2], 1)
    joined = swapped(jnp.concatenate([pair_load, wide_load], 0), "ctx", 0)
    pair_far = joined[:half_rows]
    wide_rows = jnp.concatenate([wide_load, joined[half_rows:]], 0)
    for position in range(1, doublings):
        wide_rows = jnp.concatenate([wide_rows, swapped(wide_rows, "ctx", position)], 0)
    pair_keys = jnp.concatenate([pair_parts[0], pair_far[:, 0]], 0)
    pair_values = jnp.concatenate([pair_parts[1], pair_far[:, 1]], 0)
    wide_keys = wide_rows[:, 0]
    wide_values = wide_rows[:, 1]
    local_peak, local_total, local_blend = forward_level(queries, keys_own, values_own)
    pair_peak, pair_total, pair_blend = forward_level(pair_parts[2], pair_keys, pair_values)
    wide_peak, wide_total, wide_blend = forward_level(wide_parts[2], wide_keys, wide_values)
    pair_mask = place_stats(jnp.ones_like(pair_peak), 2, pair_offsets)
    wide_mask = place_stats(jnp.ones_like(wide_peak), length, wide_offsets)
    pair_peak_full = place_stats(pair_peak, 2, pair_offsets)
    wide_peak_full = place_stats(wide_peak, length, wide_offsets)
    row_peak = jnp.maximum(local_peak, jnp.where(pair_mask > 0, pair_peak_full, local_peak))
    row_peak = jnp.maximum(row_peak, jnp.where(wide_mask > 0, wide_peak_full, local_peak))
    local_weight = jnp.exp(local_peak - row_peak)
    pair_weight = pair_mask * jnp.exp(jnp.where(pair_mask > 0, pair_peak_full, row_peak) - row_peak)
    wide_weight = wide_mask * jnp.exp(jnp.where(wide_mask > 0, wide_peak_full, row_peak) - row_peak)
    row_total = (
        local_total * local_weight
        + place_stats(pair_total, 2, pair_offsets) * pair_weight
        + place_stats(wide_total, length, wide_offsets) * wide_weight
    )
    blended = (
        local_blend * local_weight.T[:, :, None]
        + place_rows(pair_blend, 2, pair_offsets) * pair_weight.T[:, :, None]
        + place_rows(wide_blend, length, wide_offsets) * wide_weight.T[:, :, None]
    )
    attended = blended / row_total.T[:, :, None]
    log_total = row_peak + jnp.log(row_total)
    row_delta = jnp.sum(out_grads.astype(jnp.float32) * attended, axis=-1).T
    local_query, local_key, local_value = backward_level(
        queries, keys_own, values_own, out_grads, log_total, row_delta
    )
    pair_log = pick_stats(log_total, 2, pair_offsets)
    pair_delta = pick_stats(row_delta, 2, pair_offsets)
    wide_log = pick_stats(log_total, length, wide_offsets)
    wide_delta = pick_stats(row_delta, length, wide_offsets)
    pair_query_grad, pair_key_part, pair_value_part = backward_level(
        pair_parts[2], pair_keys, pair_values, pair_parts[3], pair_log, pair_delta
    )
    pair_partial = jnp.stack([pair_key_part, pair_value_part], 1)
    pair_mine = pair_partial[:half_rows] + swapped(
        pair_partial[half_rows:].astype(jnp.bfloat16), "ctx", 0
    ).astype(jnp.float32)
    pair_key_grad = pair_mine[:, 0]
    pair_value_grad = pair_mine[:, 1]
    wide_query_grad, wide_key_part, wide_value_part = backward_level(
        wide_parts[2], wide_keys, wide_values, wide_parts[3], wide_log, wide_delta
    )
    wide_buffer = jnp.stack([wide_key_part, wide_value_part], 1)
    for position in reversed(range(doublings)):
        midpoint = wide_buffer.shape[0] // 2
        wide_buffer = wide_buffer[:midpoint] + swapped(
            wide_buffer[midpoint:].astype(jnp.bfloat16), "ctx", position
        ).astype(jnp.float32)
    wide_key_grad = wide_buffer[:, 0]
    wide_value_grad = wide_buffer[:, 1]
    query_sum = (
        local_query
        + place_rows(pair_query_grad, 2, pair_offsets)
        + place_rows(wide_query_grad, length, wide_offsets)
    )
    key_sum = (
        local_key
        + place_rows(pair_key_grad, 2, pair_offsets)
        + place_rows(wide_key_grad, length, wide_offsets)
    )
    value_sum = (
        local_value
        + place_rows(pair_value_grad, 2, pair_offsets)
        + place_rows(wide_value_grad, length, wide_offsets)
    )
    width_all = head_count * head_size
    return (
        query_sum.astype(jnp.bfloat16).reshape(length, width_all),
        key_sum.astype(jnp.bfloat16).reshape(length, width_all),
        value_sum.astype(jnp.bfloat16).reshape(length, width_all),
    )


def solution(mesh):
    placed = (P("ctx", None), P("ctx", None), P("ctx", None), P("ctx", None), P())
    return jax.shard_map(
        on_device,
        mesh=mesh,
        in_specs=placed,
        out_specs=(P("ctx", None), P("ctx", None), P("ctx", None)),
        check_vma=False,
    )
```

profile of v0, /device:TPU:0, one launch (start us, length us, event | category | flops | bytes accessed | tf_op | source)
XLA Modules:
  0.0 154.7 jit_solution(1967154615015908965)
XLA Ops:
  11.8 4.6 %multiply_reduce_fusion.1 = (bf16[128,10,128]{2,1,0:T(8,128)(2,1)}, bf16[128,10,128]{2,1,0:T(8,128)(2,1)S(1)}, bf16[128,10,128]{2,1,0:T(8,128)(2,1)S(1)}, bf16[128,10,128]{2,1,0:T(8,128)(2,1)}) fusion(bf16[128,2,10,128]{3,2,1,0:T(8,128)(2,1)} %reshape_reshape.19, bf16[2,10]{1,0:T(2,128)(2,1)S(1)} %get-tuple-element.58, ...), kind=kLoop, calls=%fused_computation.54 | loop fusion | flops 1966080 | bytes 3932200 | tf_op jit(solution)/shard_map/reduce_sum | solution.py:27
  30.9 2.5 %collective-permute-start.1 = (bf16[2,2,10,128]{3,2,0,1:T(8,128)(2,1)S(1)}, bf16[2,2,10,128]{3,2,0,1:T(8,128)(2,1)S(1)}, u32[]{:S(2)}, u32[]{:S(2)}) collective-permute-start(bf16[2,2,10,128]{3,2,0,1:T(8,128)(2,1)S(1)} %pad_maximum_fusion.10), channel_id=1, source_target_pairs={{0,2},{2,0},{1,3},{3,1},{4,6},{6,4},{5,7},{7,5},{8,10},{10,8},{9,1... | collective-permute-start | bytes 30728 | tf_op jit(solution)/shard_map/ppermute | solution.py:14
  33.5 3.5 %fusion.95 = (bf16[128,1,10,128]{3,1,2,0:T(2,128)(2,1)}, bf16[128,1,10,128]{3,1,2,0:T(2,128)(2,1)}) fusion(bf16[129,2,10,128]{3,1,2,0:T(2,128)(2,1)} %collective-permute-done), kind=kLoop, calls=%fused_computation.189 | loop fusion | bytes 1310720 | tf_op jit(solution)/shard_map/slice | solution.py:111
  49.4 2.1 %collective-permute-done.3 = bf16[8,2,10,128]{3,2,0,1:T(8,128)(2,1)S(1)} collective-permute-done((bf16[8,2,10,128]{3,2,0,1:T(8,128)(2,1)S(1)}, bf16[8,2,10,128]{3,2,0,1:T(8,128)(2,1)S(1)}, u32[]{:S(2)}, u32[]{:S(2)}) %collective-permute-start.3) | collective-permute-done | bytes 40992 | tf_op jit(solution)/shard_map/ppermute | solution.py:14
  52.2 2.6 %collective-permute-start.4 = (bf16[16,2,10,128]{3,2,0,1:T(8,128)(2,1)}, bf16[16,2,10,128]{3,2,0,1:T(8,128)(2,1)}, u32[]{:S(2)}, u32[]{:S(2)}) collective-permute-start(bf16[16,2,10,128]{3,2,0,1:T(8,128)(2,1)} %get-tuple-element.34), channel_id=1, source_target_pairs={{0,16},{16,0},{1,17},{17,1},{2,18},{18,2},{3,19},{19,3},{4,20},{20... | collective-permute-start | bytes 245768 | tf_op jit(solution)/shard_map/ppermute | solution.py:14
  61.3 2.2 %copy.102 = f32[128,10,128]{2,0,1:T(8,128)} copy(f32[128,10,128]{0,2,1:T(8,128)} %convolution_bitcast_fusion.7) | data formatting | bytes 1310720 | tf_op jit(solution)/shard_map/hmn,nhc->mhc/transpose | solution.py:59
  63.4 2.6 %mul.473 = f32[128,2,10,128]{3,1,0,2:T(2,128)} broadcast(f32[128,10,128]{2,0,1:T(8,128)} %copy.102), dimensions={0,2,3} | broadcast | bytes 1966080 | tf_op jit(solution)/shard_map/mul | solution.py:33
  66.0 2.8 %copy.104 = f32[256,10,128]{0,2,1:T(8,128)} copy(f32[256,10,128]{2,0,1:T(8,128)} %bitcast.194) | data formatting | bytes 2621440 | tf_op jit(solution)/shard_map/mul | solution.py:33
  87.0 2.5 %fusion.28 = f32[256,10]{0,1:T(8,128)S(1)} fusion(f32[256,10,128]{0,2,1:T(8,128)} %copy.104, bf16[256,10,128]{0,2,1:T(8,128)(2,1)} %bitcast.192, f32[10,256,256]{1,2,0:T(8,128)S(1)} %get-tuple-element.64, f32[10,256]{1,0:T(8,128)S(1)} %get-tuple-element.63, bf16[256,10,128]{0,2,1:T(8,128)(2,1)S(1)} %bitcast.185, f32[256,10]{0,1:T(8,128)S(1)} %bitcast.230, ...), kind=kOutput, calls=%fused_computation.49 | convolution fusion | flops 173340160 | bytes 5329920 | tf_op jit(solution)/shard_map/hmn,nhc->mhc/dot_general | solution.py:59
  91.7 2.7 %fusion.55 = (f32[10]{0:T(128)S(1)}, f32[10,128]{0,1:T(8,128)}, f32[10,128]{0,1:T(8,128)}) fusion(s32[10]{0:T(128)} %copy-done.36, s32[128,2]{1,0:T(8,128)} %multiply_add_fusion, f32[10,2]{0,1:T(2,128)} %copy-done.41, f32[10,128,2]{0,2,1:T(2,128)} %bitcast.209, f32[10]{0:T(128)} %get-tuple-element.40, f32[10,128]{0,1:T(8,128)S(1)} %copy.91, ...), kind=kLoop, calls=%fused_computation.95 | loop fusion | flops 74230 | bytes 52484 | tf_op jit(solution)/shard_map/reduce_sum | solution.py:42
  97.1 2.3 %fusion.18 = bf16[10,128,256]{2,1,0:T(8,128)(2,1)S(1)} fusion(bf16[128,10,128]{0,2,1:T(8,128)(2,1)} %copy.120, f32[10,128,256]{2,1,0:T(8,128)} %copy-done, f32[10,128]{1,0:T(8,128)S(1)} %copy.113, f32[10,128]{1,0:T(8,128)S(1)} %copy.109, bf16[128,10,128]{0,2,1:T(8,128)(2,1)} %bitcast.205, bf16[128,10,128]{0,2,1:T(8,128)(2,1)} %copy.101), kind=kOutput, calls=%fused_computation.36 | convolution fusion | flops 86835200 | bytes 2959360 | tf_op jit(solution)/shard_map/mhc,nhc->hmn/dot_general | solution.py:74
  103.5 4.2 %collective-permute-done.6 = bf16[16,2,10,128]{3,2,1,0:T(8,128)(2,1)S(1)} collective-permute-done((bf16[16,2,10,128]{3,2,1,0:T(8,128)(2,1)S(1)}, bf16[16,2,10,128]{3,2,1,0:T(8,128)(2,1)S(1)}, u32[]{:S(2)}, u32[]{:S(2)}) %collective-permute-start.6) | collective-permute-done | bytes 81952 | tf_op jit(solution)/shard_map/ppermute | solution.py:14
  109.8 2.3 %collective-permute-done.7 = bf16[8,2,10,128]{3,2,1,0:T(8,128)(2,1)S(1)} collective-permute-done((bf16[8,2,10,128]{3,2,1,0:T(8,128)(2,1)S(1)}, bf16[8,2,10,128]{3,2,1,0:T(8,128)(2,1)S(1)}, u32[]{:S(2)}, u32[]{:S(2)}) %collective-permute-start.7) | collective-permute-done | bytes 40992 | tf_op jit(solution)/shard_map/ppermute | solution.py:14
  117.7 2.2 %copy.115 = f32[128,10,128]{2,0,1:T(8,128)} copy(f32[128,10,128]{0,2,1:T(8,128)} %convolution_bitcast_fusion.6) | data formatting | bytes 1310720 | tf_op jit(solution)/shard_map/hmn,nhc->mhc/transpose | solution.py:78
  119.8 2.7 %mul.505 = f32[128,2,10,128]{3,1,0,2:T(2,128)} broadcast(f32[128,10,128]{2,0,1:T(8,128)} %copy.115), dimensions={0,2,3} | broadcast | bytes 1966080 | tf_op jit(solution)/shard_map/mul | solution.py:33
  122.5 2.8 %copy.116 = f32[256,10,128]{0,2,1:T(8,128)} copy(f32[256,10,128]{2,0,1:T(8,128)} %bitcast.195) | data formatting | bytes 2621440 | tf_op jit(solution)/shard_map/mul | solution.py:33
  125.9 3.2 %fusion.17 = bf16[256,10,128]{0,2,1:T(8,128)(2,1)} fusion(bf16[256,10,128]{0,2,1:T(8,128)(2,1)} %bitcast.191, bf16[10,256,256]{1,2,0:T(8,128)(2,1)} %multiply_convert_fusion, f32[256,10,128]{0,2,1:T(8,128)} %copy.116, f32[10,128]{1,0:T(8,128)S(1)} %bitcast.226, f32[256,10]{0,1:T(8,128)S(1)} %copy-done.27, f32[256,10]{0,1:T(8,128)S(1)} %copy-done.26), kind=kOutput, calls=%fused_computation.35 | convolution fusion | flops 169410560 | bytes 3957760 | tf_op jit(solution)/shard_map/hmn,nhc->mhc/dot_general | solution.py:78
  129.1 2.2 %copy.126 = bf16[256,1280]{1,0:T(8,128)(2,1)} copy(bf16[256,1280]{0,1:T(8,128)(2,1)} %bitcast.204) | data formatting | bytes 1310720
  134.1 2.2 %copy.124 = f32[128,10,128]{2,0,1:T(8,128)} copy(f32[128,10,128]{0,2,1:T(8,128)} %get-tuple-element.28) | data formatting | bytes 1310720 | tf_op jit(solution)/shard_map/mul | solution.py:33
  136.3 2.6 %mul.523 = f32[128,2,10,128]{3,1,0,2:T(2,128)} broadcast(f32[128,10,128]{2,0,1:T(8,128)} %copy.124), dimensions={0,2,3} | broadcast | bytes 1966080 | tf_op jit(solution)/shard_map/mul | solution.py:33
  138.9 2.8 %copy.125 = f32[256,10,128]{0,2,1:T(8,128)} copy(f32[256,10,128]{2,0,1:T(8,128)} %bitcast.196) | data formatting | bytes 2621440 | tf_op jit(solution)/shard_map/mul | solution.py:33
  141.7 3.1 %fusion.16 = bf16[256,10,128]{0,2,1:T(8,128)(2,1)} fusion(bf16[256,10,128]{0,2,1:T(8,128)(2,1)S(1)} %bitcast.187, f32[10,256,256]{1,2,0:T(8,128)S(1)} %get-tuple-element.64, f32[256,10,128]{0,2,1:T(8,128)} %copy.125, f32[10,256]{1,0:T(8,128)S(1)} %copy-done.31, f32[10,128]{1,0:T(8,128)S(1)} %get-tuple-element.41, f32[256,10]{0,1:T(8,128)S(1)} %copy-done.27, ...), kind=kOutput, calls=%fused_computation.34 | convolution fusion | flops 171376640 | bytes 5278720 | tf_op jit(solution)/shard_map/hmn,mhc->nhc/dot_general | solution.py:71
  144.8 2.2 %copy.128 = bf16[256,1280]{1,0:T(8,128)(2,1)} copy(bf16[256,1280]{0,1:T(8,128)(2,1)} %bitcast.203) | data formatting | bytes 1310720
  148.7 2.9 %copy.122 = f32[256,10,128]{0,2,1:T(8,128)} copy(f32[256,10,128]{2,0,1:T(8,128)} %bitcast.197) | data formatting | bytes 2621440 | tf_op jit(solution)/shard_map/mul | solution.py:33
  (197 shorter events, 87.8 us)
Async XLA Ops:
  2.1 8.1 %copy-start.5 = (bf16[256,1280]{0,1:T(8,128)(2,1)}, bf16[256,1280]{0,1:T(8,128)(2,1)S(1)}, u32[]{:S(2)}) copy-start(bf16[256,1280]{0,1:T(8,128)(2,1)S(1)} %copy.73) | copy-start | bytes 1966084
  3.7 6.5 %copy-start.7 = (bf16[256,1280]{0,1:T(8,128)(2,1)}, bf16[256,1280]{0,1:T(8,128)(2,1)S(1)}, u32[]{:S(2)}) copy-start(bf16[256,1280]{0,1:T(8,128)(2,1)S(1)} %copy.74) | copy-start | bytes 1966084
  5.4 4.9 %copy-start.8 = (bf16[256,1280]{0,1:T(8,128)(2,1)}, bf16[256,1280]{0,1:T(8,128)(2,1)S(1)}, u32[]{:S(2)}) copy-start(bf16[256,1280]{0,1:T(8,128)(2,1)S(1)} %copy.79) | copy-start | bytes 1966084
  11.0 18.0 %copy-start.38 = (bf16[1280]{0:T(1024)(128)(2,1)}, bf16[1280]{0:T(1024)(128)(2,1)S(1)}, u32[]{:S(2)}) copy-start(bf16[1280]{0:T(1024)(128)(2,1)S(1)} %get-tuple-element.14) | copy-start | bytes 7684
  11.0 17.9 %copy-start.39 = (bf16[1280]{0:T(1024)(128)(2,1)}, bf16[1280]{0:T(1024)(128)(2,1)S(1)}, u32[]{:S(2)}) copy-start(bf16[1280]{0:T(1024)(128)(2,1)S(1)} %get-tuple-element.15) | copy-start | bytes 7684
  18.0 4.4 %copy-start.22 = (bf16[128,10,128]{2,1,0:T(8,128)(2,1)S(1)}, bf16[128,10,128]{2,1,0:T(8,128)(2,1)}, u32[]{:S(2)}) copy-start(bf16[128,10,128]{2,1,0:T(8,128)(2,1)} %get-tuple-element.19) | copy-start | bytes 983044
  18.0 11.6 %collective-permute-start = (bf16[129,2,10,128]{3,1,2,0:T(2,128)(2,1)}, bf16[129,2,10,128]{3,1,2,0:T(2,128)(2,1)}, u32[]{:S(2)}, u32[]{:S(2)}) collective-permute-start(bf16[129,2,10,128]{3,1,2,0:T(2,128)(2,1)} %copy.82), channel_id=1, source_target_pairs={{0,1},{1,0},{2,3},{3,2},{4,5},{5,4},{6,7},{7,6},{8,9},{9,8},{10,11... | collective-permute-start | bytes 1981448 | tf_op jit(solution)/shard_map/ppermute | solution.py:14
  19.0 4.4 %copy-start.41 = (f32[10,2]{0,1:T(2,128)}, f32[10,2]{0,1:T(2,128)S(1)}, u32[]{:S(2)}) copy-start(f32[10,2]{0,1:T(2,128)S(1)} %get-tuple-element.56) | copy-start | bytes 244
  26.9 4.0 %copy-start.30 = (f32[10,256]{1,0:T(8,128)}, f32[10,256]{1,0:T(8,128)S(1)}, u32[]{:S(2)}) copy-start(f32[10,256]{1,0:T(8,128)S(1)} %fusion.1) | copy-start | bytes 30724
  30.9 12.2 %collective-permute-start.1 = (bf16[2,2,10,128]{3,2,0,1:T(8,128)(2,1)S(1)}, bf16[2,2,10,128]{3,2,0,1:T(8,128)(2,1)S(1)}, u32[]{:S(2)}, u32[]{:S(2)}) collective-permute-start(bf16[2,2,10,128]{3,2,0,1:T(8,128)(2,1)S(1)} %pad_maximum_fusion.10), channel_id=1, source_target_pairs={{0,2},{2,0},{1,3},{3,1},{4,6},{6,4},{5,7},{7,5},{8,10},{10,8},{9,1... | collective-permute-start | bytes 30728 | tf_op jit(solution)/shard_map/ppermute | solution.py:14
  41.8 12.9 %copy-start = (f32[10,128,256]{2,1,0:T(8,128)}, f32[10,128,256]{2,1,0:T(8,128)S(1)}, u32[]{:S(2)}) copy-start(f32[10,128,256]{2,1,0:T(8,128)S(1)} %get-tuple-element.62) | copy-start | bytes 3932164
  43.2 4.0 %collective-permute-start.2 = (bf16[4,2,10,128]{3,2,0,1:T(8,128)(2,1)S(1)}, bf16[4,2,10,128]{3,2,0,1:T(8,128)(2,1)S(1)}, u32[]{:S(2)}, u32[]{:S(2)}) collective-permute-start(bf16[4,2,10,128]{3,2,0,1:T(8,128)(2,1)S(1)} %pad_maximum_fusion.9), channel_id=1, source_target_pairs={{0,4},{4,0},{1,5},{5,1},{2,6},{6,2},{3,7},{7,3},{8,12},{12,8},{9,1... | collective-permute-start | bytes 61448 | tf_op jit(solution)/shard_map/ppermute | solution.py:14
  47.2 4.3 %collective-permute-start.3 = (bf16[8,2,10,128]{3,2,0,1:T(8,128)(2,1)S(1)}, bf16[8,2,10,128]{3,2,0,1:T(8,128)(2,1)S(1)}, u32[]{:S(2)}, u32[]{:S(2)}) collective-permute-start(bf16[8,2,10,128]{3,2,0,1:T(8,128)(2,1)S(1)} %pad_maximum_fusion.8), channel_id=1, source_target_pairs={{0,8},{8,0},{1,9},{9,1},{2,10},{10,2},{3,11},{11,3},{4,12},{12,4},... | collective-permute-start | bytes 122888 | tf_op jit(solution)/shard_map/ppermute | solution.py:14
  52.2 16.6 %collective-permute-start.4 = (bf16[16,2,10,128]{3,2,0,1:T(8,128)(2,1)}, bf16[16,2,10,128]{3,2,0,1:T(8,128)(2,1)}, u32[]{:S(2)}, u32[]{:S(2)}) collective-permute-start(bf16[16,2,10,128]{3,2,0,1:T(8,128)(2,1)} %get-tuple-element.34), channel_id=1, source_target_pairs={{0,16},{16,0},{1,17},{17,1},{2,18},{18,2},{3,19},{19,3},{4,20},{20... | collective-permute-start | bytes 245768 | tf_op jit(solution)/shard_map/ppermute | solution.py:14
  101.0 6.7 %collective-permute-start.6 = (bf16[16,2,10,128]{3,2,1,0:T(8,128)(2,1)S(1)}, bf16[16,2,10,128]{3,2,1,0:T(8,128)(2,1)S(1)}, u32[]{:S(2)}, u32[]{:S(2)}) collective-permute-start(bf16[16,2,10,128]{3,2,1,0:T(8,128)(2,1)S(1)} %fusion.44), channel_id=1, source_target_pairs={{0,16},{16,0},{1,17},{17,1},{2,18},{18,2},{3,19},{19,3},{4,20},{20... | collective-permute-start | bytes 245768 | tf_op jit(solution)/shard_map/ppermute | solution.py:14
  101.4 7.9 %copy-start.1 = (f32[10,128,256]{2,1,0:T(8,128)S(1)}, f32[10,128,256]{2,1,0:T(8,128)}, u32[]{:S(2)}) copy-start(f32[10,128,256]{2,1,0:T(8,128)} %copy-done) | copy-start | bytes 3932164
  103.4 6.0 %copy-start.25 = (bf16[128,10,128]{0,2,1:T(8,128)(2,1)S(1)}, bf16[128,10,128]{0,2,1:T(8,128)(2,1)}, u32[]{:S(2)}) copy-start(bf16[128,10,128]{0,2,1:T(8,128)(2,1)} %copy.120) | copy-start | bytes 983044
  107.8 6.0 %copy-start.12 = (bf16[128,10,128]{0,2,1:T(8,128)(2,1)S(1)}, bf16[128,10,128]{0,2,1:T(8,128)(2,1)}, u32[]{:S(2)}) copy-start(bf16[128,10,128]{0,2,1:T(8,128)(2,1)} %copy.119) | copy-start | bytes 983044
  107.8 4.3 %collective-permute-start.7 = (bf16[8,2,10,128]{3,2,1,0:T(8,128)(2,1)S(1)}, bf16[8,2,10,128]{3,2,1,0:T(8,128)(2,1)S(1)}, u32[]{:S(2)}, u32[]{:S(2)}) collective-permute-start(bf16[8,2,10,128]{3,2,1,0:T(8,128)(2,1)S(1)} %slice.154), channel_id=1, source_target_pairs={{0,8},{8,0},{1,9},{9,1},{2,10},{10,2},{3,11},{11,3},{4,12},{12,4},... | collective-permute-start | bytes 122888 | tf_op jit(solution)/shard_map/ppermute | solution.py:14
  109.8 6.9 %copy-start.3 = (f32[256,1,10,128]{0,3,2,1:T(8,128)}, f32[256,1,10,128]{0,3,2,1:T(8,128)S(1)}, u32[]{:S(2)}) copy-start(f32[256,1,10,128]{0,3,2,1:T(8,128)S(1)} %convolution_bitcast_fusion.4) | copy-start | bytes 3932164
  112.2 4.0 %collective-permute-start.8 = (bf16[4,2,10,128]{3,2,1,0:T(8,128)(2,1)S(1)}, bf16[4,2,10,128]{3,2,1,0:T(8,128)(2,1)S(1)}, u32[]{:S(2)}, u32[]{:S(2)}) collective-permute-start(bf16[4,2,10,128]{3,2,1,0:T(8,128)(2,1)S(1)} %slice.155), channel_id=1, source_target_pairs={{0,4},{4,0},{1,5},{5,1},{2,6},{6,2},{3,7},{7,3},{8,12},{12,8},{9,1... | collective-permute-start | bytes 61448 | tf_op jit(solution)/shard_map/ppermute | solution.py:14
  116.2 9.1 %collective-permute-start.9 = (bf16[2,2,10,128]{3,2,1,0:T(8,128)(2,1)S(1)}, bf16[2,2,10,128]{3,2,1,0:T(8,128)(2,1)S(1)}, u32[]{:S(2)}, u32[]{:S(2)}) collective-permute-start(bf16[2,2,10,128]{3,2,1,0:T(8,128)(2,1)S(1)} %slice.156), channel_id=1, source_target_pairs={{0,2},{2,0},{1,3},{3,1},{4,6},{6,4},{5,7},{7,5},{8,10},{10,8},{9,1... | collective-permute-start | bytes 30728 | tf_op jit(solution)/shard_map/ppermute | solution.py:14
  125.3 6.0 %collective-permute-start.5 = (bf16[128,2,10,128]{0,3,2,1:T(8,128)(2,1)}, bf16[128,2,10,128]{0,3,2,1:T(8,128)(2,1)}, u32[]{:S(2)}, u32[]{:S(2)}) collective-permute-start(bf16[128,2,10,128]{0,3,2,1:T(8,128)(2,1)} %fusion.23), channel_id=1, source_target_pairs={{0,1},{1,0},{2,3},{3,2},{4,5},{5,4},{6,7},{7,6},{8,9},{9,8},{10,11... | collective-permute-start | bytes 1966088 | tf_op jit(solution)/shard_map/ppermute | solution.py:14
  125.3 5.9 %collective-permute-start.10 = (bf16[1,2,10,128]{3,2,1,0:T(8,128)(2,1)S(1)}, bf16[1,2,10,128]{3,2,1,0:T(8,128)(2,1)S(1)}, u32[]{:S(2)}, u32[]{:S(2)}) collective-permute-start(bf16[1,2,10,128]{3,2,1,0:T(8,128)(2,1)S(1)} %slice.157), channel_id=1, source_target_pairs={{0,1},{1,0},{2,3},{3,2},{4,5},{5,4},{6,7},{7,6},{8,9},{9,8},{10,11... | collective-permute-start | bytes 15368 | tf_op jit(solution)/shard_map/ppermute | solution.py:14
  (30 other events, 62.9 us)
where the time goes:
time: 156 us; the launch traced here: 155 us
  local copies, waits for them, and re-layouts  80 us (51%)
  matrix products  25.9 us (17%)
  other arithmetic  21.7 us (14%)
  starting transfers between devices  13.5 us (9%)
  waiting for transfers between devices  12.4 us (8%)
    mul x14, local copies, waits for them, and re-layouts, place_rows(): source[:, None] * selector[None, :, :, None]  25 us
    unnamed x98, local copies, waits for them, and re-layouts  16.4 us
    ppermute x11, starting transfers between devices, swapped(): return lax.ppermute(block, axis, route)  13.5 us
    ppermute x11, waiting for transfers between devices, swapped(): return lax.ppermute(block, axis, route)  12.4 us
    dot_general x3, matrix products, backward_level(): jnp.einsum('mhc,nhc->hmn', out_grads, values_in, preferred_element_type=j...  5.91 us
    another operation x4, local copies, waits for them, and re-layouts, pick_rows(): source.reshape(length // dilation, dilation, head_count, head_size)  5.51 us
    reduce_sum x2, other arithmetic, pick_rows(): return jnp.sum(grouped * selector[None, :, :, None], axis=1)  5.36 us
    dot_general x3, matrix products, forward_level(): jnp.einsum('hmn,nhc->mhc', powered.astype(jnp.bfloat16), values_in, prefe...  4.82 us
  transfers between devices with their start and end apart: 11, of which 5 were waited for; matrix products, arithmetic and copies ran while one was open for 34% of the time, Pallas kernels for 0%

commit v1 on v0

v1 whole, which is shorter than its diff:
```python
import functools

import jax
import jax.numpy as jnp
from jax import lax
from jax.experimental import pallas as pl
from jax.experimental.pallas import tpu as pltpu
from jax.sharding import PartitionSpec as P

NEG = -1e30
F32 = jnp.float32
BF16 = jnp.bfloat16
STAT_ROWS = 8
VMEM_LIMIT = 40 * 1024 * 1024


def iota(shape, dim):
    return lax.broadcasted_iota(jnp.int32, shape, dim)


def dot_nt(a, b):
    return lax.dot_general(a, b, (((1,), (1,)), ((), ())), preferred_element_type=F32)


def dot_tn(a, b):
    return lax.dot_general(a, b, (((0,), (0,)), ((), ())), preferred_element_type=F32)


def dot_nn(a, b):
    return lax.dot_general(a, b, (((1,), (0,)), ((), ())), preferred_element_type=F32)


def two_rows(first, second):
    row = iota((8, first.shape[1]), 0)
    return jnp.where(row == 0, first, jnp.where(row == 1, second, 0.0)).astype(BF16)


def pair_chosen(wide_offset, pair_offset):
    return jnp.bitwise_and(wide_offset, 1) == pair_offset


def pack_kernel(heads, off_ref, k_ref, v_ref, q_ref, g_ref, out_ref, buf, acc, sems):
    dh = out_ref.shape[1]
    copies = []
    for s, ref in enumerate((k_ref, v_ref, q_ref, g_ref)):
        for h in range(heads):
            base = pl.multiple_of(jnp.bitwise_and(off_ref[1, h], ~15), 16)
            slot = s * heads + h
            copy = pltpu.make_async_copy(
                ref.at[pl.ds(base, 16), pl.ds(h * dh, dh)], buf.at[slot], sems.at[slot]
            )
            copy.start()
            copies.append(copy)
    acc[...] = jnp.zeros_like(acc)
    row = iota((16, dh), 0)
    for s in range(4):
        for h in range(heads):
            slot = s * heads + h
            copies[slot].wait()
            own = row == jnp.bitwise_and(off_ref[1, h], 15)
            block = jnp.where(own, buf[slot].astype(F32), 0.0)
            acc[slot : slot + 1, :] = jnp.sum(block, axis=0, keepdims=True)
    out_ref[...] = acc[...].astype(BF16)


def stats_kernel(heads, off_ref, own_ref, far_ref, k_ref, v_ref, load_ref, s_ref, dp_ref, acc, far):
    dh = own_ref.shape[1]
    length = k_ref.shape[0]
    scale = dh**-0.5
    acc[...] = own_ref[...].astype(F32)
    far[...] = far_ref[...].astype(F32)
    row = iota((8, length), 0)
    lane = iota((8, length), 1)
    row8 = iota((8, dh), 0)
    lane8 = iota((8, dh), 1)
    table = jnp.zeros((8, dh), F32)
    for h in range(heads):
        cols = slice(h * dh, (h + 1) * dh)
        nq, ng = 2 * heads + h, 3 * heads + h
        s = dot_nt(two_rows(acc[nq : nq + 1, :], far[nq : nq + 1, :]), k_ref[:, cols]) * scale
        dp = dot_nt(two_rows(acc[ng : ng + 1, :], far[ng : ng + 1, :]), v_ref[:, cols])
        s_ref[h * 8 : h * 8 + 8, :] = s
        dp_ref[h * 8 : h * 8 + 8, :] = dp
        weight, valid = row_weights(off_ref, h, row, lane)
        masked = jnp.where(valid, s, NEG)
        m = jnp.max(masked, axis=1, keepdims=True)
        e = jnp.exp(masked - m) * weight
        t = jnp.sum(e, axis=1, keepdims=True)
        d = jnp.sum(e * dp, axis=1, keepdims=True)
        column = jnp.zeros((8, dh), F32)
        for index, value in enumerate((m[0:1], t[0:1], d[0:1], m[1:2], t[1:2], d[1:2])):
            column = jnp.where(row8 == index, value, column)
        table = jnp.where(lane8 == h, column, table)
    high = table.astype(BF16).astype(F32)
    rest = table - high
    middle = rest.astype(BF16).astype(F32)
    low = (rest - middle).astype(BF16).astype(F32)
    acc[4 * heads : 4 * heads + 8, :] = high + pltpu.roll(middle, 16, 1) + pltpu.roll(low, 32, 1)
    load = acc[...].astype(BF16)
    load_ref[...] = jnp.broadcast_to(load[None], load_ref.shape)


def row_weights(off_ref, h, row, lane):
    chosen = pair_chosen(off_ref[1, h], off_ref[0, h])
    both = jnp.logical_and(jnp.bitwise_and(lane, 1) == off_ref[0, h], chosen)
    both = both.astype(F32)
    weight = jnp.where(row == 0, 1.0 + both, jnp.where(row == 1, both, 0.0))
    return weight, weight > 0.0


def main_kernel(
    off_ref, q_ref, k_ref, v_ref, g_ref, kf_ref, vf_ref, dq_ref, dk_ref, dv_ref, ret_ref
):
    h = pl.program_id(0)
    length, dh = q_ref.shape
    half = length // 2
    scale = dh**-0.5
    pair, wide = off_ref[0, h], off_ref[1, h]
    pick = (iota((length, half), 0) == 2 * iota((length, half), 1) + pair).astype(BF16)
    q, k, v, g = q_ref[...], k_ref[...], v_ref[...], g_ref[...]
    kc = dot_tn(pick, kf_ref[...]).astype(BF16)
    vc = dot_tn(pick, vf_ref[...]).astype(BF16)
    rows = iota((length, 1), 0)
    chosen = jnp.bitwise_and(rows, 1) == pair
    a_t = chosen.astype(F32)
    a_u = (jnp.bitwise_and(iota((1, length), 1), 1) == pair).astype(F32)
    s1 = dot_nt(q, k) * scale
    s2 = dot_nt(q, kc) * scale + jnp.where(chosen, 0.0, NEG)
    m = jnp.maximum(jnp.max(s1, axis=1, keepdims=True), jnp.max(s2, axis=1, keepdims=True))
    e1 = jnp.exp(s1 - m) * (1.0 + a_t * a_u)
    e2 = jnp.exp(s2 - m)
    total = jnp.sum(e1, axis=1, keepdims=True) + jnp.sum(e2, axis=1, keepdims=True)
    inverse = jnp.where(rows == wide, 0.0, 1.0 / total)
    p1 = e1 * inverse
    p2 = e2 * inverse
    dp1 = dot_nt(g, v)
    dp2 = dot_nt(g, vc)
    delta = jnp.sum(p1 * dp1, axis=1, keepdims=True) + jnp.sum(p2 * dp2, axis=1, keepdims=True)
    ds1 = (scale * p1 * (dp1 - delta)).astype(BF16)
    ds2 = (scale * p2 * (dp2 - delta)).astype(BF16)
    dq_ref[...] = (dot_nn(ds1, k) + dot_nn(ds2, kc)).astype(BF16)
    dk_ref[...] = dot_tn(ds1, q)
    dv_ref[...] = dot_tn(p1.astype(BF16), g)
    ret_ref[:half, :] = dot_tn(ds2, q).astype(BF16)
    ret_ref[half:, :] = dot_tn(p2.astype(BF16), g).astype(BF16)


def join_kernel(off_ref, own_ref, dk_ref, dv_ref, ret_ref, kf_ref, vf_ref, dko, dvo, sc, dpc, rows):
    h = pl.program_id(0)
    heads = pl.num_programs(0)
    length, dh = dk_ref.shape
    half = length // 2
    pair = off_ref[0, h]
    pick = (iota((length, half), 0) == 2 * iota((length, half), 1) + pair).astype(BF16)
    dko[...] = dk_ref[...] + dot_nn(pick, ret_ref[:half, :])
    dvo[...] = dv_ref[...] + dot_nn(pick, ret_ref[half:, :])
    rows[...] = own_ref[...].astype(F32)
    query = rows[pl.ds(2 * heads + h, 1), :]
    grad = rows[pl.ds(3 * heads + h, 1), :]
    sc[...] = dot_nt(two_rows(query, query), kf_ref[...]) * dh**-0.5
    dpc[...] = dot_nt(two_rows(grad, grad), vf_ref[...])


def final_kernel(
    heads, span, off_ref, me_ref, recv_ref, s_ref, dp_ref, sc_ref, dpc_ref, k_ref, kf_ref,
    dqi, dki, dvi, dqo, dko, dvo, flat,
):
    length = k_ref.shape[0]
    dh = k_ref.shape[1] // heads
    slots = recv_ref.shape[1]
    scale = dh**-0.5
    me = me_ref[0]
    mate = jnp.bitwise_xor(me, 1)
    flat[...] = recv_ref[...].astype(F32).reshape(span * slots, dh)

    def gathered(slot):
        return flat[pl.ds(slot, span, stride=slots), :]

    def stat(index):
        x = gathered(4 * heads + index)
        return x + pltpu.roll(x, dh - 16, 1) + pltpu.roll(x, dh - 32, 1)

    even = jnp.bitwise_and(iota((span, dh), 0), 1) == 0

    def exchanged(x):
        return jnp.where(even, pltpu.roll(x, span - 1, 0), pltpu.roll(x, 1, 0))

    m_a, t_a, d_a = stat(0), stat(1), stat(2)
    m_b, t_b, d_b = exchanged(stat(3)), exchanged(stat(4)), exchanged(stat(5))
    m_ab = jnp.maximum(m_a, m_b)
    w_a, w_b = jnp.exp(m_a - m_ab), jnp.exp(m_b - m_ab)
    t_ab = t_a * w_a + t_b * w_b
    d_ab = d_a * w_a + d_b * w_b
    device = iota((span, 1), 0)
    is_me, is_mate = device == me, device == mate
    row = iota((8, length), 0)
    lane = iota((8, length), 1)
    row1 = iota((8, 1), 0)
    row8 = iota((8, dh), 0)

    def one(mask, x):
        return jnp.sum(jnp.where(mask, x, 0.0), axis=0, keepdims=True)

    for h in range(heads):
        cols = slice(h * dh, (h + 1) * dh)
        wide, pair = off_ref[1, h], off_ref[0, h]
        k_w, v_w, q_w, g_w = [gathered(i * heads + h) for i in range(4)]
        k_b = k_w.astype(BF16)
        s_w = dot_nt(q_w.astype(BF16), k_b) * scale
        dp_w = dot_nt(g_w.astype(BF16), v_w.astype(BF16))
        m_h = m_ab[:, h : h + 1]
        m = jnp.maximum(m_h, jnp.max(s_w, axis=1, keepdims=True))
        e = jnp.exp(s_w - m)
        shift = jnp.exp(m_h - m)
        total = t_ab[:, h : h + 1] * shift + jnp.sum(e, axis=1, keepdims=True)
        part = d_ab[:, h : h + 1] * shift + jnp.sum(e * dp_w, axis=1, keepdims=True)
        inverse = 1.0 / total
        delta = part * inverse
        p_w = e * inverse
        ds_w = (scale * p_w * (dp_w - delta)).astype(BF16).astype(F32)
        p_w = p_w.astype(BF16).astype(F32)
        mine = iota((1, span), 1) == me
        ds_column = jnp.sum(jnp.where(mine, ds_w, 0.0), axis=1, keepdims=True)
        p_column = jnp.sum(jnp.where(mine, p_w, 0.0), axis=1, keepdims=True)
        dk_w = jnp.sum(ds_column * q_w, axis=0, keepdims=True)
        dv_w = jnp.sum(p_column * g_w, axis=0, keepdims=True)
        ds_row = jnp.broadcast_to(one(is_me, ds_w), (8, span)).astype(BF16)

        def two(x):
            return jnp.where(row1 == 0, one(is_me, x), one(is_mate, x))

        m_r, inverse_r, delta_r = two(m), two(inverse), two(delta)
        weight, valid = row_weights(off_ref, h, row, lane)
        s_r = s_ref[h * 8 : h * 8 + 8, :]
        p_r = jnp.exp(jnp.where(valid, s_r - m_r, NEG)) * weight * inverse_r
        ds_r = scale * p_r * (dp_ref[h * 8 : h * 8 + 8, :] - delta_r)
        both = jnp.logical_and(jnp.bitwise_and(lane, 1) == pair, pair_chosen(wide, pair))
        s_c = sc_ref[h * 8 : h * 8 + 8, :]
        p_c = jnp.exp(jnp.where(both, s_c - m_r[0:1], NEG)) * inverse_r[0:1]
        ds_c = scale * p_c * (dpc_ref[h * 8 : h * 8 + 8, :] - delta_r[0:1])
        dq_row = (
            dot_nn(ds_r.astype(BF16), k_ref[:, cols])
            + dot_nn(ds_c.astype(BF16), kf_ref[:, cols])
            + dot_nn(ds_row, k_b)
        )[0:1, :]
        here = iota((length, dh), 0) == wide
        dqo[:, cols] = jnp.where(here, dq_row, dqi[:, cols].astype(F32)).astype(BF16)
        spot = (lane == wide).astype(F32)

        def added(base, left, first, second, own):
            high = own.astype(BF16).astype(F32)
            right = jnp.where(row8 == 2, high, jnp.where(row8 == 3, own - high, 0.0))
            right = jnp.where(row8 == 0, first, jnp.where(row8 == 1, second, right))
            left = jnp.where(row < 2, left, jnp.where(row < 4, spot, 0.0))
            return (base + dot_tn(left.astype(BF16), right.astype(BF16))).astype(BF16)

        dko[:, cols] = added(dki[:, cols], ds_r, one(is_me, q_w), one(is_mate, q_w), dk_w)
        dvo[:, cols] = added(dvi[:, cols], p_r, one(is_me, g_w), one(is_mate, g_w), dv_w)


def on_device(query, key, value, grad_out, offsets):
    length, width = query.shape
    heads = offsets.shape[1]
    dh = width // heads
    size = lax.axis_size("ctx")
    span = min(size, 128)
    slots = 4 * heads + STAT_ROWS
    half = length // 2
    mates = [(i, i ^ 1) for i in range(size)]
    vmem = pl.BlockSpec(memory_space=pltpu.VMEM)
    smem = pl.BlockSpec(memory_space=pltpu.SMEM)
    anywhere = pl.BlockSpec(memory_space=pl.ANY)
    params = pltpu.CompilerParams(vmem_limit_bytes=VMEM_LIMIT)
    small = pl.CostEstimate(flops=1000, bytes_accessed=1000, transcendentals=0)

    def shape(rows, columns, dtype):
        return jax.ShapeDtypeStruct((rows, columns), dtype)

    own = pl.pallas_call(
        functools.partial(pack_kernel, heads),
        out_shape=shape(slots, dh, BF16),
        in_specs=[smem] + [anywhere] * 4,
        out_specs=vmem,
        scratch_shapes=[
            pltpu.VMEM((4 * heads, 16, dh), BF16),
            pltpu.VMEM((slots, dh), F32),
            pltpu.SemaphoreType.DMA((4 * heads,)),
        ],
        compiler_params=params,
        cost_estimate=small,
        name="pack_rows",
    )(offsets, key, value, query, grad_out)
    far = lax.ppermute(own, "ctx", mates)
    key_far = lax.ppermute(key, "ctx", mates)
    value_far = lax.ppermute(value, "ctx", mates)
    load, s_rows, dp_rows = pl.pallas_call(
        functools.partial(stats_kernel, heads),
        out_shape=(
            jax.ShapeDtypeStruct((span, slots, dh), BF16),
            shape(heads * 8, length, F32),
            shape(heads * 8, length, F32),
        ),
        in_specs=[smem] + [vmem] * 4,
        out_specs=(vmem,) * 3,
        scratch_shapes=[pltpu.VMEM((slots, dh), F32), pltpu.VMEM((slots, dh), F32)],
        compiler_params=params,
        cost_estimate=small,
        name="row_stats",
    )(offsets, own, far, key, value)
    groups = None
    if size > span:
        groups = [list(range(base, base + span)) for base in range(0, size, span)]
    received = lax.all_to_all(load, "ctx", 0, 0, axis_index_groups=groups, tiled=True)
    block = pl.BlockSpec((length, dh), lambda h: (0, h))
    dq, dk, dv, partial = pl.pallas_call(
        main_kernel,
        grid=(heads,),
        out_shape=(
            shape(length, width, BF16),
            shape(length, width, F32),
            shape(length, width, F32),
            shape(length, width, BF16),
        ),
        in_specs=[smem] + [block] * 6,
        out_specs=(block,) * 4,
        compiler_params=params,
        cost_estimate=small,
        name="near_levels",
    )(offsets, query, key, value, grad_out, key_far, value_far)
    returned = lax.ppermute(partial, "ctx", mates)
    thin = pl.BlockSpec((8, length), lambda h: (h, 0))
    dk, dv, s_far, dp_far = pl.pallas_call(
        join_kernel,
        grid=(heads,),
        out_shape=(
            shape(length, width, F32),
            shape(length, width, F32),
            shape(heads * 8, length, F32),
            shape(heads * 8, length, F32),
        ),
        in_specs=[smem, vmem] + [block] * 5,
        out_specs=(block, block, thin, thin),
        scratch_shapes=[pltpu.VMEM((slots, dh), F32)],
        compiler_params=params,
        cost_estimate=small,
        name="join_pair",
    )(offsets, own, dk, dv, returned, key_far, value_far)
    me = lax.rem(lax.axis_index("ctx"), span).astype(jnp.int32).reshape(1)
    return pl.pallas_call(
        functools.partial(final_kernel, heads, span),
        out_shape=(shape(length, width, BF16),) * 3,
        in_specs=[smem, smem] + [vmem] * 10,
        out_specs=(vmem,) * 3,
        scratch_shapes=[pltpu.VMEM((span * slots, dh), F32)],
        compiler_params=params,
        cost_estimate=small,
        name="third_level",
    )(offsets, me, received, s_rows, dp_rows, s_far, dp_far, key, key_far, dq, dk, dv)


def solution(mesh):
    placed = (P("ctx", None), P("ctx", None), P("ctx", None), P("ctx", None), P())
    return jax.shard_map(
        on_device,
        mesh=mesh,
        in_specs=placed,
        out_specs=(P("ctx", None), P("ctx", None), P("ctx", None)),
        check_vma=False,
    )
```

time: 156 us -> 60 us (0.38)
  local copies, waits for them, and re-layouts: 80 us -> 17.2 us
  Pallas kernels: 0 us -> 29.5 us
  matrix products: 25.9 us -> 0 us
  other arithmetic: 21.7 us -> 0 us
  waiting for transfers between devices: 12.4 us -> 2.96 us
  starting transfers between devices: 13.5 us -> 8.59 us
    mul x19 -> x0, local copies, waits for them, and re-layouts: 29.6 us -> none  [the longest x14 25 us: place_rows(): source[:, None] * selector[None, :, :, None]]
    pallas_call x0 -> x5, Pallas kernels: none -> 29.5 us  [the longest x1 12.6 us: on_device(): pl.pallas_call(main_kernel, grid=(heads,), out_shape=(shape(length, width...]
    dot_general x16 -> x0, matrix products: 25.9 us -> none  [the longest x3 5.91 us: backward_level(): jnp.einsum('mhc,nhc->hmn', out_grads, values_in, preferred_element_type=j...]
    ppermute x11 -> x4, starting transfers between devices: 13.5 us -> 1.28 us  [the longest x1 0.52 us: on_device(): key_far = lax.ppermute(key, 'ctx', mates)]
    reduce_sum x6 -> x0, other arithmetic: 9.73 us -> none  [the longest x2 5.36 us: pick_rows(): return jnp.sum(grouped * selector[None, :, :, None], axis=1)]
    ppermute x11 -> x4, waiting for transfers between devices: 12.4 us -> 2.96 us  [the longest x1 2.12 us: on_device(): returned = lax.ppermute(partial, 'ctx', mates)]
    reduce_sum x8 -> x0, local copies, waits for them, and re-layouts: 7.43 us -> none  [the longest x4 4.03 us: pick_rows(): return jnp.sum(grouped * selector[None, :, :, None], axis=1)]
    all_to_all x0 -> x1, starting transfers between devices: none -> 7.3 us  [on_device(): lax.all_to_all(load, 'ctx', 0, 0, axis_index_groups=groups, tiled=True)]
  transfers between devices with their start and end apart: 11 -> 5, of which waited for: 5 -> 2; matrix products, arithmetic and copies ran while one was open for 34% -> 0% of each run, Pallas kernels for 0% -> 36%
where the time goes in v1:
time: 60 us; the launch traced here: 59.1 us
  Pallas kernels  29.5 us (49%)
  local copies, waits for them, and re-layouts  17.2 us (29%)
  starting transfers between devices  8.59 us (14%)
  waiting for transfers between devices  2.96 us (5%)
  between operations  0.77 us (1%)
    unnamed x46, local copies, waits for them, and re-layouts  17.2 us
    pallas_call x1, Pallas kernels, on_device(): pl.pallas_call(main_kernel, grid=(heads,), out_shape=(shape(length, width...  12.6 us
    pallas_call x1, Pallas kernels, on_device(): pl.pallas_call(functools.partial(final_kernel, heads, span), out_shape=(s...  8.12 us
    all_to_all x1, starting transfers between devices, on_device(): lax.all_to_all(load, 'ctx', 0, 0, axis_index_groups=groups, tiled=True)  7.3 us
    pallas_call x1, Pallas kernels, on_device(): pl.pallas_call(join_kernel, grid=(heads,), out_shape=(shape(length, width...  5.89 us
    ppermute x1, waiting for transfers between devices, on_device(): returned = lax.ppermute(partial, 'ctx', mates)  2.12 us
    pallas_call x1, Pallas kernels, on_device(): pl.pallas_call(functools.partial(pack_kernel, heads), out_shape=shape(slo...  1.66 us
    pallas_call x1, Pallas kernels, on_device(): pl.pallas_call(functools.partial(stats_kernel, heads), out_shape=(jax.Sha...  1.25 us
  transfers between devices with their start and end apart: 5, of which 2 were waited for; matrix products, arithmetic and copies ran while one was open for 0% of the time, Pallas kernels for 36%

profile of v1, /device:TPU:0, one launch (start us, length us, event | category | flops | bytes accessed | tf_op | source)
XLA Modules:
  0.0 59.1 jit_solution(12202246785464623903)
XLA Ops:
  1.2 1.1 %copy-done = bf16[256,1280]{1,0:T(8,128)(2,1)S(1)} copy-done((bf16[256,1280]{1,0:T(8,128)(2,1)S(1)}, bf16[256,1280]{1,0:T(8,128)(2,1)}, u32[]{:S(2)}) %copy-start) | copy-done | bytes 655384
  2.3 1.1 %copy-done.2 = bf16[256,1280]{1,0:T(8,128)(2,1)S(1)} copy-done((bf16[256,1280]{1,0:T(8,128)(2,1)S(1)}, bf16[256,1280]{1,0:T(8,128)(2,1)}, u32[]{:S(2)}) %copy-start.2) | copy-done | bytes 655384
  3.4 1.1 %copy-done.4 = bf16[256,1280]{1,0:T(8,128)(2,1)S(1)} copy-done((bf16[256,1280]{1,0:T(8,128)(2,1)S(1)}, bf16[256,1280]{1,0:T(8,128)(2,1)}, u32[]{:S(2)}) %copy-start.4) | copy-done | bytes 655384
  4.5 1.1 %copy-done.6 = bf16[256,1280]{1,0:T(8,128)(2,1)S(1)} copy-done((bf16[256,1280]{1,0:T(8,128)(2,1)S(1)}, bf16[256,1280]{1,0:T(8,128)(2,1)}, u32[]{:S(2)}) %copy-start.6) | copy-done | bytes 655384
  5.6 0.7 %copy-done.21 = s32[2,10]{1,0:T(2,128)S(1)} copy-done((s32[2,10]{1,0:T(2,128)S(1)}, s32[2,10]{1,0:T(2,128)}, u32[]{:S(2)}) %copy-start.21) | copy-done | bytes 104
  6.3 1.7 %pack_rows.1.own_ref = bf16[48,128]{1,0:T(8,128)(2,1)S(1)} custom-call(s32[2,10]{1,0:T(2,128)S(1)} %copy-done.21, bf16[256,1280]{1,0:T(8,128)(2,1)S(1)} %copy-done, bf16[256,1280]{1,0:T(8,128)(2,1)S(1)} %copy-done.2, bf16[256,1280]{1,0:T(8,128)(2,1)S(1)} %copy-done.4, bf16[256,1280]{1,0:T(8,128)(2,1)S(1)} %copy-done.6), custom_call_target="tpu_custom_call" | custom-call | flops 1000 | bytes 1000 | tf_op jit(solution)/shard_map/pack_rows/pallas_call | solution.py:279
  8.5 0.8 %collective-permute-done.far_ref = bf16[48,128]{1,0:T(8,128)(2,1)S(1)} collective-permute-done((bf16[48,128]{1,0:T(8,128)(2,1)S(1)}, bf16[48,128]{1,0:T(8,128)(2,1)S(1)}, u32[]{:S(2)}, u32[]{:S(2)}) %collective-permute-start) | collective-permute-done | bytes 12320 | tf_op jit(solution)/shard_map/ppermute | solution.py:293
  9.3 1.3 %row_stats.1 = (bf16[32,48,128]{2,1,0:T(8,128)(2,1)S(1)}, f32[80,256]{1,0:T(8,128)S(1)}, f32[80,256]{1,0:T(8,128)S(1)}) custom-call(s32[2,10]{1,0:T(2,128)S(1)} %copy-done.22, bf16[48,128]{1,0:T(8,128)(2,1)S(1)} %pack_rows.1.own_ref, bf16[48,128]{1,0:T(8,128)(2,1)S(1)} %collective-permute-done.far_ref, bf16[256,1280]{1,0:T(8,128)(2,1)S(1)} %copy-done, ...), custom_call_target="tpu_custom_call" | custom-call | flops 1000 | bytes 1000 | tf_op jit(solution)/shard_map/row_stats/pallas_call | solution.py:296
  10.6 0.7 %copy-done.18 = bf16[32,48,128]{2,1,0:T(8,128)(2,1)} copy-done((bf16[32,48,128]{2,1,0:T(8,128)(2,1)}, bf16[32,48,128]{2,1,0:T(8,128)(2,1)S(1)}, u32[]{:S(2)}) %copy-start.18) | copy-done | bytes 393240
  11.3 7.3 %all-to-all-start = ((bf16[32,48,128]{2,1,0:T(8,128)(2,1)}), bf16[32,48,128]{2,1,0:T(8,128)(2,1)}, u32[]{:S(2)}, u32[]{:S(2)}) async-start(bf16[32,48,128]{2,1,0:T(8,128)(2,1)} %copy-done.18), calls=%async_computation | async-start | bytes 786432 | tf_op jit(solution)/shard_map/all_to_all | solution.py:313
  18.7 12.6 %near_levels.1 = (bf16[256,1280]{1,0:T(8,128)(2,1)S(1)}, f32[256,1280]{1,0:T(8,128)S(1)}, f32[256,1280]{1,0:T(8,128)S(1)}, bf16[256,1280]{1,0:T(8,128)(2,1)}) custom-call(s32[2,10]{1,0:T(2,128)S(1)} %copy-done.22, bf16[256,1280]{1,0:T(8,128)(2,1)S(1)} %copy-done.5, bf16[256,1280]{1,0:T(8,128)(2,1)S(1)} %copy-done.1, bf16[256,1280]{1,0:T(8,128)(2,1)S(1)} %copy-done.3, ...), custom_call_target="tpu_custom_call" | custom-call | flops 1000 | bytes 1000 | tf_op jit(solution)/shard_map/near_levels/pallas_call | solution.py:315
  31.3 1.1 %copy-done.8 = f32[256,1280]{1,0:T(8,128)} copy-done((f32[256,1280]{1,0:T(8,128)}, f32[256,1280]{1,0:T(8,128)S(1)}, u32[]{:S(2)}) %copy-start.8) | copy-done | bytes 1310744
  32.3 1.1 %copy-done.10 = f32[256,1280]{1,0:T(8,128)} copy-done((f32[256,1280]{1,0:T(8,128)}, f32[256,1280]{1,0:T(8,128)S(1)}, u32[]{:S(2)}) %copy-start.10) | copy-done | bytes 1310744
  33.4 0.8 %copy-done.14 = bf16[256,1280]{1,0:T(8,128)(2,1)} copy-done((bf16[256,1280]{1,0:T(8,128)(2,1)}, bf16[256,1280]{1,0:T(8,128)(2,1)S(1)}, u32[]{:S(2)}) %copy-start.14) | copy-done | bytes 655384
  34.4 2.1 %collective-permute-done.3.ret_ref = bf16[256,1280]{1,0:T(8,128)(2,1)S(1)} collective-permute-done((bf16[256,1280]{1,0:T(8,128)(2,1)}, bf16[256,1280]{1,0:T(8,128)(2,1)S(1)}, u32[]{:S(2)}, u32[]{:S(2)}) %collective-permute-start.3) | collective-permute-done | bytes 655392 | tf_op jit(solution)/shard_map/ppermute | solution.py:330
  36.6 0.8 %copy-done.16 = bf16[256,1280]{1,0:T(8,128)(2,1)} copy-done((bf16[256,1280]{1,0:T(8,128)(2,1)}, bf16[256,1280]{1,0:T(8,128)(2,1)S(1)}, u32[]{:S(2)}) %copy-start.16) | copy-done | bytes 655384
  37.4 1.3 %copy-done.9 = f32[256,1280]{1,0:T(8,128)S(1)} copy-done((f32[256,1280]{1,0:T(8,128)S(1)}, f32[256,1280]{1,0:T(8,128)}, u32[]{:S(2)}) %copy-start.9) | copy-done | bytes 1310744
  38.7 1.3 %copy-done.11 = f32[256,1280]{1,0:T(8,128)S(1)} copy-done((f32[256,1280]{1,0:T(8,128)S(1)}, f32[256,1280]{1,0:T(8,128)}, u32[]{:S(2)}) %copy-start.11) | copy-done | bytes 1310744
  40.0 1.1 %copy-done.17 = bf16[256,1280]{1,0:T(8,128)(2,1)S(1)} copy-done((bf16[256,1280]{1,0:T(8,128)(2,1)S(1)}, bf16[256,1280]{1,0:T(8,128)(2,1)}, u32[]{:S(2)}) %copy-start.17) | copy-done | bytes 655384
  41.1 5.9 %join_pair.1 = (f32[256,1280]{1,0:T(8,128)S(1)}, f32[256,1280]{1,0:T(8,128)S(1)}, f32[80,256]{1,0:T(8,128)S(1)}, f32[80,256]{1,0:T(8,128)S(1)}) custom-call(s32[2,10]{1,0:T(2,128)S(1)} %copy-done.22, bf16[48,128]{1,0:T(8,128)(2,1)S(1)} %pack_rows.1.own_ref, f32[256,1280]{1,0:T(8,128)S(1)} %copy-done.9, f32[256,1280]{1,0:T(8,128)S(1)} %copy-done.11, ...), custom_call_target="tpu_custom_call" | custom-call | flops 1000 | bytes 1000 | tf_op jit(solution)/shard_map/join_pair/pallas_call | solution.py:332
  47.0 1.1 %copy-done.12 = f32[256,1280]{1,0:T(8,128)} copy-done((f32[256,1280]{1,0:T(8,128)}, f32[256,1280]{1,0:T(8,128)S(1)}, u32[]{:S(2)}) %copy-start.12) | copy-done | bytes 1310744
  48.7 1.3 %copy-done.13 = f32[256,1280]{1,0:T(8,128)S(1)} copy-done((f32[256,1280]{1,0:T(8,128)S(1)}, f32[256,1280]{1,0:T(8,128)}, u32[]{:S(2)}) %copy-start.13) | copy-done | bytes 1310744
  50.1 0.9 %copy-done.20 = f32[80,256]{1,0:T(8,128)S(1)} copy-done((f32[80,256]{1,0:T(8,128)S(1)}, f32[80,256]{1,0:T(8,128)}, u32[]{:S(2)}) %copy-start.20) | copy-done | bytes 81944
  50.9 8.1 %third_level.1 = (bf16[256,1280]{1,0:T(8,128)(2,1)}, bf16[256,1280]{1,0:T(8,128)(2,1)}, bf16[256,1280]{1,0:T(8,128)(2,1)}) custom-call(s32[2,10]{1,0:T(2,128)S(1)} %copy-done.22, s32[1]{0:T(128)} %bitcast.me_ref, bf16[32,48,128]{2,1,0:T(8,128)(2,1)} %all-to-all-done.recv_ref, f32[80,256]{1,0:T(8,128)S(1)} %get-tuple-element.15.s_ref, ...), custom_call_target="tpu_custom_call" | custom-call | flops 1000 | bytes 1000 | tf_op jit(solution)/shard_map/third_level/pallas_call | solution.py:349
  (37 shorter events, 2.0 us)
Async XLA Ops:
  0.6 18.0 %collective-permute-start.1 = (bf16[256,1280]{1,0:T(8,128)(2,1)}, bf16[256,1280]{1,0:T(8,128)(2,1)S(1)}, u32[]{:S(2)}, u32[]{:S(2)}) collective-permute-start(bf16[256,1280]{1,0:T(8,128)(2,1)} %k_ref.7), channel_id=1, source_target_pairs={{0,1},{1,0},{2,3},{3,2},{4,5},{5,4},{6,7},{7,6},{8,9},{9,8},{10,11... | collective-permute-start | bytes 1966088 | tf_op jit(solution)/shard_map/ppermute | solution.py:294
  1.1 17.5 %collective-permute-start.2 = (bf16[256,1280]{1,0:T(8,128)(2,1)}, bf16[256,1280]{1,0:T(8,128)(2,1)}, u32[]{:S(2)}, u32[]{:S(2)}) collective-permute-start(bf16[256,1280]{1,0:T(8,128)(2,1)} %v_ref.5), channel_id=1, source_target_pairs={{0,1},{1,0},{2,3},{3,2},{4,5},{5,4},{6,7},{7,6},{8,9},{9,8},{10,11... | collective-permute-start | bytes 1966088 | tf_op jit(solution)/shard_map/ppermute | solution.py:295
  1.2 1.1 %copy-start = (bf16[256,1280]{1,0:T(8,128)(2,1)S(1)}, bf16[256,1280]{1,0:T(8,128)(2,1)}, u32[]{:S(2)}) copy-start(bf16[256,1280]{1,0:T(8,128)(2,1)} %k_ref.7) | copy-start | bytes 1966084
  2.3 1.1 %copy-start.2 = (bf16[256,1280]{1,0:T(8,128)(2,1)S(1)}, bf16[256,1280]{1,0:T(8,128)(2,1)}, u32[]{:S(2)}) copy-start(bf16[256,1280]{1,0:T(8,128)(2,1)} %v_ref.5) | copy-start | bytes 1966084
  3.4 1.1 %copy-start.4 = (bf16[256,1280]{1,0:T(8,128)(2,1)S(1)}, bf16[256,1280]{1,0:T(8,128)(2,1)}, u32[]{:S(2)}) copy-start(bf16[256,1280]{1,0:T(8,128)(2,1)} %q_ref.3) | copy-start | bytes 1966084
  4.5 1.1 %copy-start.6 = (bf16[256,1280]{1,0:T(8,128)(2,1)S(1)}, bf16[256,1280]{1,0:T(8,128)(2,1)}, u32[]{:S(2)}) copy-start(bf16[256,1280]{1,0:T(8,128)(2,1)} %g_ref.3) | copy-start | bytes 1966084
  6.3 3.0 %copy-start.22 = (s32[2,10]{1,0:T(2,128)S(1)}, s32[2,10]{1,0:T(2,128)}, u32[]{:S(2)}) copy-start(s32[2,10]{1,0:T(2,128)} %off_ref.9) | copy-start | bytes 244
  6.3 12.4 %copy-start.7 = (bf16[256,1280]{1,0:T(8,128)(2,1)S(1)}, bf16[256,1280]{1,0:T(8,128)(2,1)}, u32[]{:S(2)}) copy-start(bf16[256,1280]{1,0:T(8,128)(2,1)} %g_ref.3) | copy-start | bytes 1966084
  7.9 10.7 %copy-start.1 = (bf16[256,1280]{1,0:T(8,128)(2,1)S(1)}, bf16[256,1280]{1,0:T(8,128)(2,1)}, u32[]{:S(2)}) copy-start(bf16[256,1280]{1,0:T(8,128)(2,1)} %k_ref.7) | copy-start | bytes 1966084
  7.9 10.7 %copy-start.3 = (bf16[256,1280]{1,0:T(8,128)(2,1)S(1)}, bf16[256,1280]{1,0:T(8,128)(2,1)}, u32[]{:S(2)}) copy-start(bf16[256,1280]{1,0:T(8,128)(2,1)} %v_ref.5) | copy-start | bytes 1966084
  8.0 10.7 %copy-start.5 = (bf16[256,1280]{1,0:T(8,128)(2,1)S(1)}, bf16[256,1280]{1,0:T(8,128)(2,1)}, u32[]{:S(2)}) copy-start(bf16[256,1280]{1,0:T(8,128)(2,1)} %q_ref.3) | copy-start | bytes 1966084
  8.0 1.3 %collective-permute-start = (bf16[48,128]{1,0:T(8,128)(2,1)S(1)}, bf16[48,128]{1,0:T(8,128)(2,1)S(1)}, u32[]{:S(2)}, u32[]{:S(2)}) collective-permute-start(bf16[48,128]{1,0:T(8,128)(2,1)S(1)} %pack_rows.1.own_ref), channel_id=1, source_target_pairs={{0,1},{1,0},{2,3},{3,2},{4,5},{5,4},{6,7},{7,6},{8,9},{9,8},{10,11... | collective-permute-start | bytes 36872 | tf_op jit(solution)/shard_map/ppermute | solution.py:293
  11.3 37.4 %all-to-all-start = ((bf16[32,48,128]{2,1,0:T(8,128)(2,1)}), bf16[32,48,128]{2,1,0:T(8,128)(2,1)}, u32[]{:S(2)}, u32[]{:S(2)}) async-start(bf16[32,48,128]{2,1,0:T(8,128)(2,1)} %copy-done.18), calls=%async_computation | async-start | bytes 786432 | tf_op jit(solution)/shard_map/all_to_all | solution.py:313
  31.3 1.1 %copy-start.8 = (f32[256,1280]{1,0:T(8,128)}, f32[256,1280]{1,0:T(8,128)S(1)}, u32[]{:S(2)}) copy-start(f32[256,1280]{1,0:T(8,128)S(1)} %get-tuple-element.17.dk_ref) | copy-start | bytes 3932164
  32.3 1.1 %copy-start.10 = (f32[256,1280]{1,0:T(8,128)}, f32[256,1280]{1,0:T(8,128)S(1)}, u32[]{:S(2)}) copy-start(f32[256,1280]{1,0:T(8,128)S(1)} %get-tuple-element.18.dv_ref) | copy-start | bytes 3932164
  34.2 2.3 %collective-permute-start.3 = (bf16[256,1280]{1,0:T(8,128)(2,1)}, bf16[256,1280]{1,0:T(8,128)(2,1)S(1)}, u32[]{:S(2)}, u32[]{:S(2)}) collective-permute-start(bf16[256,1280]{1,0:T(8,128)(2,1)} %get-tuple-element.19), channel_id=1, source_target_pairs={{0,1},{1,0},{2,3},{3,2},{4,5},{5,4},{6,7},{7,6},{8,9},{9,8},{10,11... | collective-permute-start | bytes 1966088 | tf_op jit(solution)/shard_map/ppermute | solution.py:330
  36.6 0.8 %copy-start.16 = (bf16[256,1280]{1,0:T(8,128)(2,1)}, bf16[256,1280]{1,0:T(8,128)(2,1)S(1)}, u32[]{:S(2)}) copy-start(bf16[256,1280]{1,0:T(8,128)(2,1)S(1)} %collective-permute-done.3.ret_ref) | copy-start | bytes 1966084
  37.4 1.3 %copy-start.9 = (f32[256,1280]{1,0:T(8,128)S(1)}, f32[256,1280]{1,0:T(8,128)}, u32[]{:S(2)}) copy-start(f32[256,1280]{1,0:T(8,128)} %copy-done.8) | copy-start | bytes 3932164
  38.7 1.3 %copy-start.11 = (f32[256,1280]{1,0:T(8,128)S(1)}, f32[256,1280]{1,0:T(8,128)}, u32[]{:S(2)}) copy-start(f32[256,1280]{1,0:T(8,128)} %copy-done.10) | copy-start | bytes 3932164
  40.0 1.1 %copy-start.17 = (bf16[256,1280]{1,0:T(8,128)(2,1)S(1)}, bf16[256,1280]{1,0:T(8,128)(2,1)}, u32[]{:S(2)}) copy-start(bf16[256,1280]{1,0:T(8,128)(2,1)} %copy-done.16) | copy-start | bytes 1966084
  41.1 7.6 %copy-start.15 = (bf16[256,1280]{1,0:T(8,128)(2,1)S(1)}, bf16[256,1280]{1,0:T(8,128)(2,1)}, u32[]{:S(2)}) copy-start(bf16[256,1280]{1,0:T(8,128)(2,1)} %copy-done.14) | copy-start | bytes 1966084
  47.0 1.1 %copy-start.12 = (f32[256,1280]{1,0:T(8,128)}, f32[256,1280]{1,0:T(8,128)S(1)}, u32[]{:S(2)}) copy-start(f32[256,1280]{1,0:T(8,128)S(1)} %get-tuple-element.24.dvi) | copy-start | bytes 3932164
  48.7 1.3 %copy-start.13 = (f32[256,1280]{1,0:T(8,128)S(1)}, f32[256,1280]{1,0:T(8,128)}, u32[]{:S(2)}) copy-start(f32[256,1280]{1,0:T(8,128)} %copy-done.12) | copy-start | bytes 3932164
  50.1 0.9 %copy-start.20 = (f32[80,256]{1,0:T(8,128)S(1)}, f32[80,256]{1,0:T(8,128)}, u32[]{:S(2)}) copy-start(f32[80,256]{1,0:T(8,128)} %copy-done.19) | copy-start | bytes 245764
  (4 other events, 2.9 us)
